TPU v7x, 128 devices: a whole 4x4x4 slice. The times are simulated.
128 devices in a mesh: stream: 16 (over z, y), cross: 8 (over x, core).
Axes of the slice: x: 4, y: 4, z: 4, core: 2. Of those that a mesh axis runs over, the one named last changes fastest.
Arguments:
- flow_state: float32 [16, 8, 12, 64, 256], P('stream', 'cross'), may hold values from 0.04 to 7.2, as said below
- flux_blocks: bfloat16 [16, 8, 7, 64, 64, 256], P('stream', 'cross'), may hold values from -0.25 to 0.25
- block_links: int32 [16, 8, 7, 256], P('stream', 'cross'), may hold values from 0 to 255
- face_cells: int32 [16, 8, 4, 1536], P('stream', 'cross'), may hold values from 0 to 16383
- face_weight: float32 [16, 8, 4, 1536], P('stream', 'cross'), may hold values from 0.05 to 0.5
- point_owner: int32 [16, 8, 32768], P('stream', 'cross'), may hold values from 0 to 8, as said below
- point_slot: int32 [16, 8, 32768], P('stream', 'cross'), may hold values from 0 to 127, as said below
- point_block: int32 [16, 8, 32768], P('stream', 'cross'), may hold values from 0 to 255
- point_weight: bfloat16 [16, 8, 64, 32768], P('stream', 'cross'), may hold values from 0 to 0.03125
- point_area: float32 [16, 8, 32768], P('stream', 'cross'), may hold values from 0.1 to 1
- pellet_gain: float32 [16, 8, 9, 128], P('stream', 'cross'), may hold values from 0.3 to 3
Outputs:
- next_state: float32 [16, 8, 12, 64, 256], P('stream', 'cross')
- pellet_rate: float32 [16, 8, 9, 128], P('stream', 'cross')
Inputs may be any that keep to these rules, and one draw needn't show every extreme that they name: `flow_state`: values at every size stay within the range; each tile has its own level per component. `point_owner`: code 3 a + c names the tile at offset (a - 1, c - 1) along stream and cross; it never names a tile outside the bed; the first 128 points of every tile have code 4. `point_slot`: the first 128 points of every tile have slot equal to their position, so every owned pellet has points on its own tile.
All inputs are finite; a program needn't handle non-finite values.
Results may differ from a plain program's by a relative error of at most 0.0003.
The roundings to bfloat16 on the way count: a program that leaves them out, or rounds other values in their place, can miss the bound.
Values sent between devices are 32-bit elements; how exact they have to be, the bound alone decides.
A program may use at most 128 MiB of HBM per device.

v0:
```python
import math

import jax
import jax.numpy as jnp
from jax import lax
from jax.sharding import PartitionSpec as P

R = 9
PEL = 128


phase_dt = 0.5
highest = lax.Precision.HIGHEST


def passed_along(block, axis, distance):
    devices = range(lax.axis_size(axis))
    route = [(i - distance, i) for i in devices if i - distance in devices]
    return lax.ppermute(block, axis, route)


def padded(block, sides, width):
    for axis, dim in sides:
        count = lax.axis_size(axis)
        forward = [(i, i + 1) for i in range(count - 1)]
        backward = [(target, source) for source, target in forward]
        low = lax.ppermute(
            lax.slice_in_dim(block, block.shape[dim] - width, None, axis=dim), axis, forward
        )
        high = lax.ppermute(lax.slice_in_dim(block, 0, width, axis=dim), axis, backward)
        block = jnp.concatenate([low, block, high], axis=dim)
    return block


def pass_faces_stream(values, offset):
    return passed_along(values, "stream", offset)


def pass_faces_cross(values, offset):
    return passed_along(values, "cross", offset)


def shards(
    flow_state,
    flux_blocks,
    block_links,
    face_cells,
    face_weight,
    point_owner,
    point_slot,
    point_block,
    point_weight,
    point_area,
    pellet_gain,
):
    state = flow_state[0, 0]
    components, cell_rows, blocks = state.shape
    cell_ids = face_cells[0, 0]
    face_gain = face_weight[0, 0]
    sides, faces = cell_ids.shape
    all_faces = sides * faces
    face_list = cell_ids.reshape(all_faces)
    face_len = math.gcd(all_faces, 1024)
    face_count = all_faces // face_len
    state_rows = state.reshape(components * cell_rows, blocks)
    block_column = lax.broadcasted_iota(jnp.int32, (blocks, 1), 0)
    cell_column = lax.broadcasted_iota(jnp.int32, (cell_rows, 1), 0)

    def face_tables(which):
        face_here = lax.dynamic_slice_in_dim(face_list, which * face_len, face_len)
        block_table = (face_here[None, :] % blocks == block_column).astype(jnp.float32)
        cell_table = (face_here[None, :] // blocks == cell_column).astype(jnp.float32)
        return (block_table, cell_table)

    def face_pick(which):
        block_table, cell_table = face_tables(which)
        chosen = jnp.dot(state_rows, block_table, precision=highest)
        chosen = chosen.reshape(components, cell_rows, face_len)
        return jnp.sum(chosen * cell_table[None], axis=1)

    face_values = lax.map(face_pick, jnp.arange(face_count, dtype=jnp.int32))
    face_values = face_values.transpose(1, 0, 2).reshape(components, sides, faces)
    outgoing = face_gain[None] * face_values
    from_lower = pass_faces_stream(outgoing[:, 1], 1)
    from_upper = pass_faces_stream(outgoing[:, 0], -1)
    from_left = pass_faces_cross(outgoing[:, 3], 1)
    from_right = pass_faces_cross(outgoing[:, 2], -1)
    incoming = jnp.stack([from_lower, from_upper, from_left, from_right], axis=1)
    net = (incoming - outgoing).reshape(components, all_faces)
    rounded = state.astype(jnp.bfloat16)
    links = block_links[0, 0]
    slots = links.shape[0]
    link_table = (links.reshape(1, slots * blocks) == block_column).astype(jnp.bfloat16)
    gathered = jnp.dot(
        rounded.reshape(components * cell_rows, blocks),
        link_table,
        preferred_element_type=jnp.float32,
    )
    gathered = gathered.astype(jnp.bfloat16).reshape(components, cell_rows, slots, blocks)
    interior = jnp.einsum(
        "kijb,qjkb->qib", flux_blocks[0, 0], gathered, preferred_element_type=jnp.float32
    )
    interp = point_weight[0, 0]
    block_ids = point_block[0, 0]
    area = point_area[0, 0]
    points = block_ids.shape[0]
    step_len = math.gcd(points, 2048)
    number = points // step_len
    reacting = rounded[:R].reshape(R * cell_rows, blocks)
    block_iota = lax.broadcasted_iota(jnp.int32, (1, blocks), 1)
    bin_count = 9 * PEL
    bin_iota = lax.broadcasted_iota(jnp.int32, (1, bin_count), 1)
    bins = point_owner[0, 0] * PEL + point_slot[0, 0]

    def interpolate(carry, which):
        first = which * step_len
        ids_here = lax.dynamic_slice_in_dim(block_ids, first, step_len)
        onehot = (ids_here[:, None] == block_iota).astype(jnp.bfloat16)
        picked = lax.dot_general(
            reacting, onehot, (((1,), (1,)), ((), ())), preferred_element_type=jnp.float32
        )
        weights_here = lax.dynamic_slice_in_dim(interp, first, step_len, 1).astype(jnp.float32)
        values = jnp.sum(picked.reshape(R, cell_rows, step_len) * weights_here[None], axis=1)
        area_here = lax.dynamic_slice_in_dim(area, first, step_len)
        stacked = jnp.concatenate([values * area_here[None], area_here[None]], axis=0)
        bins_here = lax.dynamic_slice_in_dim(bins, first, step_len)
        bin_table = (bins_here[:, None] == bin_iota).astype(jnp.float32)
        return (carry + jnp.dot(stacked, bin_table, precision=highest), None)

    binned, _ = lax.scan(
        interpolate, jnp.zeros((R + 1, bin_count), jnp.float32), jnp.arange(number, dtype=jnp.int32)
    )
    partial_value = binned.reshape(R + 1, 3, 3, PEL).transpose(1, 2, 0, 3)
    widened = padded(partial_value, (("stream", 0), ("cross", 1)), 1)
    totals = jnp.sum(widened[0::2, 0::2], axis=(0, 1))
    mean = totals[:R] / totals[R : R + 1]
    rates_out = pellet_gain[0, 0] * mean / jnp.sqrt(1.0 + mean * mean)
    neighbour_rates = padded(rates_out[None, None], (("stream", 0), ("cross", 1)), 1)
    lookup = neighbour_rates.reshape(9, R, PEL).transpose(1, 0, 2).reshape(R, bin_count)

    def deposit(carry, which):
        first = which * step_len
        ids_here = lax.dynamic_slice_in_dim(block_ids, first, step_len)
        onehot = (ids_here[:, None] == block_iota).astype(jnp.bfloat16)
        weights_here = lax.dynamic_slice_in_dim(interp, first, step_len, 1).astype(jnp.float32)
        bins_here = lax.dynamic_slice_in_dim(bins, first, step_len)
        bin_table = (bins_here[:, None] == bin_iota).astype(jnp.float32)
        rate_here = lax.dot_general(lookup, bin_table, (((1,), (1,)), ((), ())), precision=highest)
        source_here = lax.dynamic_slice_in_dim(area, first, step_len)[None] * rate_here
        spread = (weights_here[None] * source_here[:, None, :]).astype(jnp.bfloat16)
        spread = spread.reshape(R * cell_rows, step_len)
        return (carry + jnp.dot(spread, onehot, preferred_element_type=jnp.float32), None)

    surface, _ = lax.scan(
        deposit,
        jnp.zeros((R * cell_rows, blocks), jnp.float32),
        jnp.arange(number, dtype=jnp.int32),
    )
    whole = jnp.concatenate(
        [
            surface.reshape(R, cell_rows, blocks),
            jnp.zeros((components - R, cell_rows, blocks), jnp.float32),
        ],
        axis=0,
    )

    def face_add(carry, which):
        block_table, cell_table = face_tables(which)
        net_here = lax.dynamic_slice_in_dim(net, which * face_len, face_len, 1)
        masked = (net_here[:, None, :] * cell_table[None]).reshape(components * cell_rows, face_len)
        added = lax.dot_general(masked, block_table, (((1,), (1,)), ((), ())), precision=highest)
        return (carry + added, None)

    face_term, _ = lax.scan(
        face_add,
        jnp.zeros((components * cell_rows, blocks), jnp.float32),
        jnp.arange(face_count, dtype=jnp.int32),
    )
    next_state = state + phase_dt * (
        interior + face_term.reshape(components, cell_rows, blocks) + whole
    )
    return (next_state[None, None], rates_out[None, None])


def solution(mesh):
    placed = (
        P("stream", "cross", None, None, None),
        P("stream", "cross", None, None, None, None),
        P("stream", "cross", None, None),
        P("stream", "cross", None, None),
        P("stream", "cross", None, None),
        P("stream", "cross", None),
        P("stream", "cross", None),
        P("stream", "cross", None),
        P("stream", "cross", None, None),
        P("stream", "cross", None),
        P("stream", "cross", None, None),
    )
    return jax.shard_map(
        shards,
        mesh=mesh,
        in_specs=placed,
        out_specs=(P("stream", "cross", None, None, None), P("stream", "cross", None, None)),
        check_vma=False,
    )
```

profile of v0, /device:TPU:1, one launch (start us, length us, event | category | flops | bytes accessed | tf_op | source)
XLA Modules:
  0.0 538.5 jit_solution(16427342276943202231)
XLA Ops:
  6.2 151.4 %while.50 = (s32[]{:T(128)}, f32[10,1152]{1,0:T(8,128)}, s32[16]{0:T(128)S(1)}, s32[32768]{0:T(1024)}, bf16[576,256]{1,0:T(8,128)(2,1)S(1)}, /*index=5*/bf16[64,...) while((s32[]{:T(128)}, f32[10,1152]{1,0:T(8,128)}, ...), condition=%wide.region_7.8_spmd.clone, body=%wide.region_5.7_spmd.clone.sunk | while | flops 892512768 | bytes 11880713 | solution.py:130
  159.2 4.0 collective-permute-start.4
  164.6 23.4 %while.48 = (s32[]{:T(128)}, f32[6,12,1024]{2,1,0:T(8,128)}, s32[6]{0:T(128)S(1)}, s32[6144]{0:T(1024)S(1)}, f32[768,256]{1,0:T(8,128)S(1)}, /*index=5*/s32[]{:T(128)}, s32[1]{0:T(128)}, s32[]{:T(128)}, s32[]{:T(128)}) while((s32[]{:T(128)}, f32[6,12,1024]{2,1,0:T(8,128)}, s32[6]{0:T(128)S(1)}, s32[6144]{0:T(1024)S(1)}, ...), condition=%wide.region_2.3_spmd.clone, body=%wide.region_0.2_spmd.clone.sunk | while | flops 2417898496 | bytes 7792811 | solution.py:81
  190.8 4.0 collective-permute-start.6
  201.4 10.5 %slice.45 = f32[3,3,10,128]{3,1,0,2:T(4,128)S(1)} slice(f32[5,5,10,128]{3,1,0,2:T(8,128)} %pad_maximum_fusion.1), slice={[0:5:2], [0:5:2], [0:10:1], [0:128:1]} | slice | bytes 92160 | tf_op jit(solution)/shard_map/slice | solution.py:135
  212.1 4.3 collective-permute-start.8
  228.3 4.0 collective-permute-done.9
  234.7 3.6 collective-permute-start.10
  245.1 9.3 %reshape.212 = bf16[12,64,7,256]{1,0,3,2:T(8,128)(2,1)} reshape(bf16[768,1792]{0,1:T(8,128)(2,1)} %fusion.43) | data formatting | bytes 5505024 | tf_op jit(solution)/shard_map/reshape | solution.py:99
  254.4 40.5 %copy.41 = bf16[7,64,64,256]{2,1,0,3:T(8,128)(2,1)} copy(bf16[7,64,64,256]{3,2,1,0:T(8,128)(2,1)} %bitcast.132) | data formatting | bytes 29360128 | tf_op jit(solution)/shard_map/squeeze | solution.py:101
  294.9 4.3 collective-permute-start
  302.2 180.2 %while.51 = (s32[]{:T(128)}, f32[576,256]{1,0:T(8,128)}, s32[16]{0:T(128)S(1)}, bf16[64,32768]{1,0:T(8,128)(2,1)}, f32[32768]{0:T(1024)}, /*index=5*/s32[32768]{...) while((s32[]{:T(128)}, f32[576,256]{1,0:T(8,128)}, ...), condition=%wide.region_10.11_spmd.clone, body=%wide.region_9.10_spmd.clone.sunk | while | flops 864471040 | bytes 12190473 | solution.py:154
  304.8 5.2 fusion.89
  316.1 5.2 fusion.89
  327.4 5.2 fusion.89
  338.6 5.2 fusion.89
  349.9 5.2 fusion.89
  361.1 5.2 fusion.89
  372.4 5.2 fusion.89
  383.7 5.2 fusion.89
  394.9 5.2 fusion.89
  406.2 5.2 fusion.89
  417.4 5.2 fusion.89
  428.7 5.2 fusion.89
  440.0 5.2 fusion.89
  451.2 5.2 fusion.89
  462.5 5.2 fusion.89
  473.7 5.2 fusion.89
  482.3 3.5 copy.51
  488.2 27.4 %while.49 = (s32[]{:T(128)}, f32[768,256]{1,0:T(8,128)S(1)}, s32[6]{0:T(128)S(1)}, f32[12,6144]{1,0:T(8,128)}, s32[6144]{0:T(1024)S(1)}, /*index=5*/s32[]{:T(128)}, s32[1]{0:T(128)}, s32[]{:T(128)}, s32[]{:T(128)}) while((s32[]{:T(128)}, f32[768,256]{1,0:T(8,128)S(1)}, s32[6]{0:T(128)S(1)}, f32[12,6144]{1,0:T(8,128)}, ...), condition=%wide.region_4.5_spmd.clone, body=%wide.region_3.4_spmd.clone.sunk | while | flops 2417514496 | bytes 8562869 | solution.py:174
  518.0 17.3 %fusion.47 = f32[1,1,12,64,256]{3,2,4,1,0:T(8,128)} fusion(f32[12,64,256]{1,0,2:T(8,128)} %copy.48, f32[9,64,256]{1,0,2:T(8,128)} %copy.51, bf16[7,64,64,256]{2,1,0,3:T(8,128)(2,1)} %copy.41, bf16[12,64,7,256]{1,0,3,2:T(8,128)(2,1)} %reshape.212, f32[1,1,12,64,256]{3,2,4,1,0:T(8,128)S(1)} %copy.38), kind=kOutput, calls=%fused_computation.72 | convolution fusion | flops 176947200 | bytes 20381696 | tf_op jit(solution)/shard_map/kijb,qjkb->qib/dot_general | solution.py:100
  535.3 3.2 copy.52
  (554 shorter events, 315.6 us)
Async XLA Ops:
  6.2 158.3 %copy-start.9 = (s32[1,1,4,1536]{3,2,1,0:T(4,128)S(1)}, s32[1,1,4,1536]{3,2,1,0:T(4,128)}, u32[]{:S(2)}) copy-start(s32[1,1,4,1536]{3,2,1,0:T(4,128)} %param.22) | copy-start | bytes 73732
  6.2 158.3 %copy-start = (f32[1,1,12,64,256]{4,3,2,1,0:T(8,128)S(1)}, f32[1,1,12,64,256]{4,3,2,1,0:T(8,128)}, u32[]{:S(2)}) copy-start(f32[1,1,12,64,256]{4,3,2,1,0:T(8,128)} %param.19) | copy-start | bytes 2359300
  159.2 30.8 %collective-permute-start.4 = (f32[1,3,10,128]{3,1,0,2:T(4,128)}, f32[1,3,10,128]{3,1,0,2:T(4,128)S(1)}, u32[]{:S(2)}, u32[]{:S(2)}) collective-permute-start(f32[1,3,10,128]{3,1,0,2:T(4,128)} %get-tuple-element.467), channel_id=1, source_target_pairs={{0,8},{8,16},{16,24},{24,32},{32,40},{40,48},{48,56},{56,64},{64,7... | collective-permute-start | bytes 46088 | tf_op jit(solution)/shard_map/ppermute | solution.py:27
  163.2 26.8 %collective-permute-start.5 = (f32[1,3,10,128]{3,1,0,2:T(4,128)}, f32[1,3,10,128]{3,1,0,2:T(4,128)}, u32[]{:S(2)}, u32[]{:S(2)}) collective-permute-start(f32[1,3,10,128]{3,1,0,2:T(4,128)} %get-tuple-element.468), channel_id=1, source_target_pairs={{8,0},{16,8},{24,16},{32,24},{40,32},{48,40},{56,48},{64,56},{72,6... | collective-permute-start | bytes 46088 | tf_op jit(solution)/shard_map/ppermute | solution.py:30
  164.6 32.2 %copy-start.5 = (f32[1,1,4,1536]{3,2,1,0:T(4,128)S(1)}, f32[1,1,4,1536]{3,2,1,0:T(4,128)}, u32[]{:S(2)}) copy-start(f32[1,1,4,1536]{3,2,1,0:T(4,128)} %param.23) | copy-start | bytes 73732
  164.6 47.5 %copy-start.12 = (f32[1,1,9,128]{3,1,2,0:T(1,128)S(1)}, f32[1,1,9,128]{3,1,2,0:T(1,128)}, u32[]{:S(2)}) copy-start(f32[1,1,9,128]{3,1,2,0:T(1,128)} %param.29) | copy-start | bytes 13828
  187.9 39.0 %copy-start.10 = (s32[1,1,7,256]{3,1,2,0:T(1,128)S(1)}, s32[1,1,7,256]{3,1,2,0:T(1,128)}, u32[]{:S(2)}) copy-start(s32[1,1,7,256]{3,1,2,0:T(1,128)} %param.21) | copy-start | bytes 21508
  190.8 7.6 %collective-permute-start.6 = (f32[5,1,10,128]{3,1,0,2:T(1,128)S(1)}, f32[5,1,10,128]{3,1,0,2:T(1,128)S(1)}, u32[]{:S(2)}, u32[]{:S(2)}) collective-permute-start(f32[5,1,10,128]{3,1,0,2:T(1,128)S(1)} %get-tuple-element.465), channel_id=1, source_target_pairs={{0,1},{1,2},{2,3},{3,4},{4,5},{5,6},{6,7},{8,9},{9,10},{10,11},{11... | collective-permute-start | bytes 76808 | tf_op jit(solution)/shard_map/ppermute | solution.py:27
  194.8 5.2 collective-permute-start.7
  212.1 33.0 %copy-start.11 = (f32[1,1,9,128]{3,1,2,0:T(1,128)}, f32[1,1,9,128]{3,1,2,0:T(1,128)S(1)}, u32[]{:S(2)}) copy-start(f32[1,1,9,128]{3,1,2,0:T(1,128)S(1)} %broadcast_in_dim.42) | copy-start | bytes 13828
  212.1 16.2 %collective-permute-start.8 = (f32[1,1,9,128]{3,1,2,0:T(1,128)S(1)}, f32[1,1,9,128]{3,1,2,0:T(1,128)S(1)}, u32[]{:S(2)}, u32[]{:S(2)}) collective-permute-start(f32[1,1,9,128]{3,1,2,0:T(1,128)S(1)} %broadcast_in_dim.42), channel_id=1, source_target_pairs={{0,8},{8,16},{16,24},{24,32},{32,40},{40,48},{48,56},{56,64},{64,7... | collective-permute-start | bytes 13832 | tf_op jit(solution)/shard_map/ppermute | solution.py:27
  219.4 266.4 %collective-permute-start.2 = (f32[12,1536]{1,0:T(8,128)}, f32[12,1536]{1,0:T(8,128)}, u32[]{:S(2)}, u32[]{:S(2)}) collective-permute-start(f32[12,1536]{1,0:T(8,128)} %bitcast.86), channel_id=1, source_target_pairs={{0,1},{1,2},{2,3},{3,4},{4,5},{5,6},{6,7},{8,9},{9,10},{10,11},{11... | collective-permute-start | bytes 221192 | tf_op jit(solution)/shard_map/ppermute | solution.py:19
  222.5 263.4 %collective-permute-start.3 = (f32[12,1536]{1,0:T(8,128)}, f32[12,1536]{1,0:T(8,128)}, u32[]{:S(2)}, u32[]{:S(2)}) collective-permute-start(f32[12,1536]{1,0:T(8,128)} %bitcast.89), channel_id=1, source_target_pairs={{1,0},{2,1},{3,2},{4,3},{5,4},{6,5},{7,6},{9,8},{10,9},{11,10},{12... | collective-permute-start | bytes 221192 | tf_op jit(solution)/shard_map/ppermute | solution.py:19
  225.7 260.2 %collective-permute-start.1 = (f32[12,1536]{1,0:T(8,128)}, f32[12,1536]{1,0:T(8,128)}, u32[]{:S(2)}, u32[]{:S(2)}) collective-permute-start(f32[12,1536]{1,0:T(8,128)} %bitcast.87), channel_id=1, source_target_pairs={{8,0},{16,8},{24,16},{32,24},{40,32},{48,40},{56,48},{64,56},{72,6... | collective-permute-start | bytes 221192 | tf_op jit(solution)/shard_map/ppermute | solution.py:19
  227.0 5.4 collective-permute-start.9
  232.4 62.5 %collective-permute-start.11 = (f32[3,1,9,128]{3,1,2,0:T(1,128)S(1)}, f32[3,1,9,128]{3,1,2,0:T(1,128)S(1)}, u32[]{:S(2)}, u32[]{:S(2)}) collective-permute-start(f32[3,1,9,128]{3,1,2,0:T(1,128)S(1)} %constant_dynamic-update-slice_fusion), channel_id=1, source_target_pairs={{1,0},{2,1},{3,2},{4,3},{5,4},{6,5},{7,6},{9,8},{10,9},{11,10},{12... | collective-permute-start | bytes 41480 | tf_op jit(solution)/shard_map/ppermute | solution.py:30
  234.7 64.5 %collective-permute-start.10 = (f32[3,1,9,128]{3,1,2,0:T(1,128)S(1)}, f32[3,1,9,128]{3,1,2,0:T(1,128)}, u32[]{:S(2)}, u32[]{:S(2)}) collective-permute-start(f32[3,1,9,128]{3,1,2,0:T(1,128)S(1)} %constant_dynamic-update-slice_fusion), channel_id=1, source_target_pairs={{0,1},{1,2},{2,3},{3,4},{4,5},{5,6},{6,7},{8,9},{9,10},{10,11},{11... | collective-permute-start | bytes 41480 | tf_op jit(solution)/shard_map/ppermute | solution.py:27
  294.9 190.9 %collective-permute-start = (f32[12,1536]{1,0:T(8,128)}, f32[12,1536]{1,0:T(8,128)}, u32[]{:S(2)}, u32[]{:S(2)}) collective-permute-start(f32[12,1536]{1,0:T(8,128)} %bitcast.152), channel_id=1, source_target_pairs={{0,8},{8,16},{16,24},{24,32},{32,40},{40,48},{48,56},{56,64},{64,7... | collective-permute-start | bytes 221192 | tf_op jit(solution)/shard_map/ppermute | solution.py:19
  304.8 6.7 %copy-start.1 = (f32[576,256]{1,0:T(8,128)S(1)}, f32[576,256]{1,0:T(8,128)}, u32[]{:S(2)}) copy-start(f32[576,256]{1,0:T(8,128)} %get-tuple-element.740) | copy-start | bytes 1769476 | tf_op jit(solution)/shard_map/while
  316.1 6.7 %copy-start.1 = (f32[576,256]{1,0:T(8,128)S(1)}, f32[576,256]{1,0:T(8,128)}, u32[]{:S(2)}) copy-start(f32[576,256]{1,0:T(8,128)} %get-tuple-element.740) | copy-start | bytes 1769476 | tf_op jit(solution)/shard_map/while
  327.4 6.7 %copy-start.1 = (f32[576,256]{1,0:T(8,128)S(1)}, f32[576,256]{1,0:T(8,128)}, u32[]{:S(2)}) copy-start(f32[576,256]{1,0:T(8,128)} %get-tuple-element.740) | copy-start | bytes 1769476 | tf_op jit(solution)/shard_map/while
  338.6 6.7 %copy-start.1 = (f32[576,256]{1,0:T(8,128)S(1)}, f32[576,256]{1,0:T(8,128)}, u32[]{:S(2)}) copy-start(f32[576,256]{1,0:T(8,128)} %get-tuple-element.740) | copy-start | bytes 1769476 | tf_op jit(solution)/shard_map/while
  349.9 6.7 %copy-start.1 = (f32[576,256]{1,0:T(8,128)S(1)}, f32[576,256]{1,0:T(8,128)}, u32[]{:S(2)}) copy-start(f32[576,256]{1,0:T(8,128)} %get-tuple-element.740) | copy-start | bytes 1769476 | tf_op jit(solution)/shard_map/while
  361.1 6.7 %copy-start.1 = (f32[576,256]{1,0:T(8,128)S(1)}, f32[576,256]{1,0:T(8,128)}, u32[]{:S(2)}) copy-start(f32[576,256]{1,0:T(8,128)} %get-tuple-element.740) | copy-start | bytes 1769476 | tf_op jit(solution)/shard_map/while
  372.4 6.7 %copy-start.1 = (f32[576,256]{1,0:T(8,128)S(1)}, f32[576,256]{1,0:T(8,128)}, u32[]{:S(2)}) copy-start(f32[576,256]{1,0:T(8,128)} %get-tuple-element.740) | copy-start | bytes 1769476 | tf_op jit(solution)/shard_map/while
  383.7 6.7 %copy-start.1 = (f32[576,256]{1,0:T(8,128)S(1)}, f32[576,256]{1,0:T(8,128)}, u32[]{:S(2)}) copy-start(f32[576,256]{1,0:T(8,128)} %get-tuple-element.740) | copy-start | bytes 1769476 | tf_op jit(solution)/shard_map/while
  394.9 6.7 %copy-start.1 = (f32[576,256]{1,0:T(8,128)S(1)}, f32[576,256]{1,0:T(8,128)}, u32[]{:S(2)}) copy-start(f32[576,256]{1,0:T(8,128)} %get-tuple-element.740) | copy-start | bytes 1769476 | tf_op jit(solution)/shard_map/while
  406.2 6.7 %copy-start.1 = (f32[576,256]{1,0:T(8,128)S(1)}, f32[576,256]{1,0:T(8,128)}, u32[]{:S(2)}) copy-start(f32[576,256]{1,0:T(8,128)} %get-tuple-element.740) | copy-start | bytes 1769476 | tf_op jit(solution)/shard_map/while
  417.4 6.7 %copy-start.1 = (f32[576,256]{1,0:T(8,128)S(1)}, f32[576,256]{1,0:T(8,128)}, u32[]{:S(2)}) copy-start(f32[576,256]{1,0:T(8,128)} %get-tuple-element.740) | copy-start | bytes 1769476 | tf_op jit(solution)/shard_map/while
  428.7 6.7 %copy-start.1 = (f32[576,256]{1,0:T(8,128)S(1)}, f32[576,256]{1,0:T(8,128)}, u32[]{:S(2)}) copy-start(f32[576,256]{1,0:T(8,128)} %get-tuple-element.740) | copy-start | bytes 1769476 | tf_op jit(solution)/shard_map/while
  440.0 6.7 %copy-start.1 = (f32[576,256]{1,0:T(8,128)S(1)}, f32[576,256]{1,0:T(8,128)}, u32[]{:S(2)}) copy-start(f32[576,256]{1,0:T(8,128)} %get-tuple-element.740) | copy-start | bytes 1769476 | tf_op jit(solution)/shard_map/while
  451.2 6.7 %copy-start.1 = (f32[576,256]{1,0:T(8,128)S(1)}, f32[576,256]{1,0:T(8,128)}, u32[]{:S(2)}) copy-start(f32[576,256]{1,0:T(8,128)} %get-tuple-element.740) | copy-start | bytes 1769476 | tf_op jit(solution)/shard_map/while
  (53 other events, 66.7 us)
where the time goes:
time: 549 us; the launch traced here: 539 us
  matrix products  210 us (38%)
  local copies, waits for them, and re-layouts  196 us (36%)
  other arithmetic  62.8 us (11%)
  starting transfers between devices  33.1 us (6%)
  loops' own time  29.5 us (5%)
  waiting for transfers between devices  5.55 us (1%)
    dot_general x16, matrix products, deposit(): lax.dot_general(lookup, bin_table, (((1,), (1,)), ((), ())), precision=hi...  83.8 us
    dot_general x16, matrix products, interpolate(): return (carry + jnp.dot(stacked, bin_table, precision=highest), None)  48.8 us
    squeeze x1, local copies, waits for them, and re-layouts, shards(): flux_blocks[0, 0]  40.5 us
    while x128, local copies, waits for them, and re-layouts  25.6 us
    dynamic_slice x32, local copies, waits for them, and re-layouts, shards(): lax.scan(interpolate, jnp.zeros((R + 1, bin_count), jnp.float32), jnp.ara...  20.2 us
    dot_general x16, matrix products, interpolate(): lax.dot_general(reacting, onehot, (((1,), (1,)), ((), ())), preferred_ele...  19.6 us
    dot_general x1, matrix products, shards(): jnp.einsum('kijb,qjkb->qib', flux_blocks[0, 0], gathered, preferred_eleme...  17.3 us
    dot_general x16, matrix products, deposit(): jnp.dot(spread, onehot, preferred_element_type=jnp.float32)  16.8 us
  transfers between devices with their start and end apart: 12, of which 2 were waited for; matrix products, arithmetic and copies ran while one was open for 46% of the time, Pallas kernels for 0%

commit v1 on v0

v1 whole, which is shorter than its diff:
```python
import functools

import jax
import jax.numpy as jnp
from jax import lax
from jax.experimental import pallas as pl
from jax.experimental.pallas import tpu as pltpu
from jax.sharding import PartitionSpec as P

R = 9
PEL = 128
GROUP = 16
POINT_STEP = 2048
FACE_STEP = 1536
OWNER_PAIRS = 5
ROWS = 16

phase_dt = 0.5
f32 = jnp.float32
bf16 = jnp.bfloat16
OFFSETS = [(a, c) for a in range(3) for c in range(3)]
AROUND = [n for n in range(9) if n != 4]


def one_hot(row, count):
    ids = row.astype(f32).astype(bf16)
    iota = lax.broadcasted_iota(jnp.int32, (count, row.shape[1]), 0).astype(f32).astype(bf16)
    return jnp.where(iota == ids, bf16(1), bf16(0))


def split(values):
    high = values.astype(bf16)
    return high, (values - high.astype(f32)).astype(bf16)


def dot(a, b):
    return jnp.dot(a, b, preferred_element_type=f32)


def dot_t(a, b):
    return lax.dot_general(a, b, (((1,), (1,)), ((), ())), preferred_element_type=f32)


def kernel(
    stream_count,
    cross_count,
    state_hbm, flux_hbm, links_hbm, cells_hbm, face_gain_hbm, owner_hbm, slot_hbm, block_hbm,
    weight_hbm, area_hbm, gain_hbm,
    next_ref, rates_ref,
    state_ref, flux_ref, links_ref, cells_ref, face_gain_ref, owner_ref, slot_ref, block_ref,
    weight_ref, area_ref, gain_ref,
    split_ref, coupled_ref, grouped_ref, total_ref,
    face_out, face_in, part_out, part_in, rate_out, rate_in, binned_ref, table_ref,
    in_sem, face_send, face_recv, part_send, part_recv, rate_send, rate_recv,
):
    s, x = lax.axis_index("stream"), lax.axis_index("cross")
    components, cell_rows, blocks = state_ref.shape
    rows = components * cell_rows
    slots = flux_ref.shape[0]
    points = block_ref.shape[1]
    faces = face_gain_ref.shape[1] // 4

    def at(first, second):
        return (
            lax.rem(s + (first + stream_count), stream_count),
            lax.rem(x + (second + cross_count), cross_count),
        )

    pairs = [
        (state_hbm, state_ref), (cells_hbm, cells_ref), (face_gain_hbm, face_gain_ref),
        (block_hbm, block_ref), (owner_hbm, owner_ref), (slot_hbm, slot_ref), (area_hbm, area_ref),
        (weight_hbm, weight_ref), (links_hbm, links_ref), (gain_hbm, gain_ref), (flux_hbm, flux_ref),
    ]
    loads = [pltpu.make_async_copy(a, b, in_sem.at[n]) for n, (a, b) in enumerate(pairs)]
    for load in loads:
        load.start()
    barrier = pltpu.get_barrier_semaphore()
    for n in AROUND:
        a, c = OFFSETS[n]
        pl.semaphore_signal(
            barrier, inc=1, device_id=at(a - 1, c - 1), device_id_type=pl.DeviceIdType.MESH
        )

    for load in loads[:3]:
        load.wait()
    high, low = split(state_ref[...].reshape(rows, blocks))
    split_ref[0:rows] = high
    split_ref[rows:2 * rows] = low
    cell_iota = lax.broadcasted_iota(jnp.int32, (cell_rows, FACE_STEP), 0)

    def gather_faces(side, carry):
        first = pl.multiple_of(side * faces, 128)
        ids = cells_ref[0:1, pl.ds(first, FACE_STEP)]
        table = one_hot(ids % blocks, blocks)
        both = dot(split_ref[...], table)
        chosen = both[:rows] + both[rows:]
        here = jnp.where((ids // blocks == cell_iota)[None], chosen.reshape(components, cell_rows, -1), 0.0)
        gain = face_gain_ref[0:1, pl.ds(first, FACE_STEP)]
        face_out[side, 0:components] = jnp.sum(here, axis=1) * gain
        face_out[side, components:ROWS] = jnp.zeros((ROWS - components, FACE_STEP), f32)
        return carry

    lax.fori_loop(0, 4, gather_faces, 0)
    pl.semaphore_wait(barrier, len(AROUND))
    sides = [(-1, 0, 1), (1, 0, 0), (0, -1, 3), (0, 1, 2)]
    face_copies = [
        pltpu.make_async_remote_copy(
            src_ref=face_out.at[d],
            dst_ref=face_in.at[opposite],
            send_sem=face_send.at[d],
            recv_sem=face_recv.at[opposite],
            device_id=at(da, dc),
            device_id_type=pl.DeviceIdType.MESH,
        )
        for d, (da, dc, opposite) in enumerate(sides)
    ]
    for copy in face_copies:
        copy.start()

    for load in loads[3:8]:
        load.wait()
    binned_ref[...] = jnp.zeros_like(binned_ref)

    def pellet_code(first):
        owner = owner_ref[0:1, pl.ds(first, POINT_STEP)]
        slot = slot_ref[0:1, pl.ds(first, POINT_STEP)]
        return owner // 2, one_hot((owner % 2) * PEL + slot, 2 * PEL)

    def interpolate(step, carry):
        first = pl.multiple_of(step * POINT_STEP, POINT_STEP)
        table = one_hot(block_ref[0:1, pl.ds(first, POINT_STEP)], blocks)
        picked = dot(split_ref[0:R * cell_rows], table).reshape(R, cell_rows, POINT_STEP)
        weights = weight_ref[:, pl.ds(first, POINT_STEP)].astype(f32)
        values = jnp.sum(picked * weights[None], axis=1)
        area = area_ref[0:1, pl.ds(first, POINT_STEP)]
        stacked = jnp.concatenate(
            [values * area, area, jnp.zeros((ROWS - R - 1, POINT_STEP), f32)], axis=0
        )
        high, low = split(stacked)
        pair, pellets = pellet_code(first)
        both = jnp.concatenate([high.astype(f32), low.astype(f32)], axis=0)
        masked = jnp.concatenate([jnp.where(pair == g, both, 0.0) for g in range(OWNER_PAIRS)], axis=0)
        binned_ref[...] += dot_t(masked.astype(bf16), pellets)
        return carry

    lax.fori_loop(0, points // POINT_STEP, interpolate, 0)
    for n in range(9):
        first = (n // 2) * 2 * ROWS
        lanes = slice((n % 2) * PEL, (n % 2 + 1) * PEL)
        part_out[n] = (
            binned_ref[first:first + ROWS, lanes] + binned_ref[first + ROWS:first + 2 * ROWS, lanes]
        )
    part_copies = [
        pltpu.make_async_remote_copy(
            src_ref=part_out.at[n],
            dst_ref=part_in.at[n],
            send_sem=part_send.at[n],
            recv_sem=part_recv.at[n],
            device_id=at(OFFSETS[n][0] - 1, OFFSETS[n][1] - 1),
            device_id_type=pl.DeviceIdType.MESH,
        )
        for n in AROUND
    ]
    for copy in part_copies:
        copy.start()

    for load in loads[8:]:
        load.wait()
    groups = blocks // GROUP
    width = components * GROUP

    for k in range(slots):
        table = one_hot(links_ref[k:k + 1, :], blocks)
        coupled = dot(split_ref[0:rows], table).astype(bf16).reshape(components, cell_rows, blocks)
        for g in range(groups):
            lanes = slice(g * GROUP, (g + 1) * GROUP)
            coupled_ref[g, k * cell_rows:(k + 1) * cell_rows, 0:width] = jnp.concatenate(
                [coupled[q, :, lanes] for q in range(components)], axis=1
            )

    step = 8
    mask = (
        lax.broadcasted_iota(jnp.int32, (1, GROUP, width), 2) % GROUP
        == lax.broadcasted_iota(jnp.int32, (1, GROUP, width), 1)
    )

    def couple(which, carry):
        first = pl.multiple_of(which * step, step)
        turned = [
            jnp.transpose(flux_ref[:, first + n].reshape(slots * cell_rows, blocks)) for n in range(step)
        ]
        for g in range(groups):
            left = jnp.concatenate([t[g * GROUP:(g + 1) * GROUP] for t in turned], axis=0)
            product = dot(left, coupled_ref[g, :, 0:width]).reshape(step, GROUP, width)
            grouped_ref[g, pl.ds(first, step), 0:width] = jnp.sum(jnp.where(mask, product, 0.0), axis=1)
        return carry

    lax.fori_loop(0, cell_rows // step, couple, 0)

    totals = part_out[4]
    for copy in part_copies:
        copy.wait()
    for n in AROUND:
        totals = totals + part_in[n]
    mean = totals[0:R] / totals[R:R + 1]
    rates = gain_ref[...] * mean / jnp.sqrt(1.0 + mean * mean)
    rates_ref[...] = rates
    rate_out[0:R] = rates
    rate_out[R:ROWS] = jnp.zeros((ROWS - R, PEL), f32)
    rate_copies = [
        pltpu.make_async_remote_copy(
            src_ref=rate_out,
            dst_ref=rate_in.at[n],
            send_sem=rate_send.at[n],
            recv_sem=rate_recv.at[n],
            device_id=at(1 - OFFSETS[n][0], 1 - OFFSETS[n][1]),
            device_id_type=pl.DeviceIdType.MESH,
        )
        for n in AROUND
    ]
    for copy in rate_copies:
        copy.start()

    for q in range(components):
        total_ref[q * cell_rows:(q + 1) * cell_rows] = jnp.concatenate(
            [grouped_ref[g, :, q * GROUP:(q + 1) * GROUP] for g in range(groups)], axis=1
        )
    for copy in face_copies:
        copy.wait()
    inside = [s > 0, s < stream_count - 1, x > 0, x < cross_count - 1]
    present = [jnp.where(here, 1.0, 0.0) for here in inside]
    for d in range(4):
        face_in[d] = face_in[d] * present[d] - face_out[d]

    def add_faces(side, carry):
        first = pl.multiple_of(side * faces, 128)
        ids = cells_ref[0:1, pl.ds(first, FACE_STEP)]
        table = one_hot(ids % blocks, blocks)
        here = ids // blocks == cell_iota
        net = face_in[side, 0:components]
        spread = jnp.where(here[None], net[:, None, :], 0.0).reshape(rows, FACE_STEP)
        high, low = split(spread)
        total_ref[...] += dot_t(high, table) + dot_t(low, table)
        return carry

    lax.fori_loop(0, 4, add_faces, 0)

    rate_in[4] = rate_out[...]
    for copy in rate_copies:
        copy.wait()
    for n in range(9):
        first = (n // 2) * 2 * ROWS
        lanes = slice((n % 2) * PEL, (n % 2 + 1) * PEL)
        high, low = split(rate_in[n])
        table_ref[first:first + ROWS, lanes] = high
        table_ref[first + ROWS:first + 2 * ROWS, lanes] = low
    table_ref[8 * ROWS:10 * ROWS, PEL:2 * PEL] = jnp.zeros((2 * ROWS, PEL), bf16)

    def deposit(step, carry):
        first = pl.multiple_of(step * POINT_STEP, POINT_STEP)
        pair, pellets = pellet_code(first)
        found = dot(table_ref[...], pellets)
        source = jnp.zeros((ROWS, POINT_STEP), f32)
        for g in range(OWNER_PAIRS):
            top = g * 2 * ROWS
            rate = found[top:top + ROWS] + found[top + ROWS:top + 2 * ROWS]
            source = jnp.where(pair == g, rate, source)
        source = source * area_ref[0:1, pl.ds(first, POINT_STEP)]
        table = one_hot(block_ref[0:1, pl.ds(first, POINT_STEP)], blocks)
        weights = weight_ref[:, pl.ds(first, POINT_STEP)].astype(f32)
        spread = (weights[None] * source[0:R, None, :]).astype(bf16).reshape(R * cell_rows, POINT_STEP)
        total_ref[0:R * cell_rows] += dot_t(spread, table)
        return carry

    lax.fori_loop(0, points // POINT_STEP, deposit, 0)
    next_ref[...] = state_ref[...] + phase_dt * total_ref[...].reshape(components, cell_rows, blocks)


def shards(mesh_shape, *arrays):
    arrays = [array[0, 0] for array in arrays]
    (state, flux, links, cells, face_gain, owner, slot, block, weight, area, gain) = arrays
    components, cell_rows, blocks = state.shape
    slots = flux.shape[0]
    rows = components * cell_rows
    cells = cells.reshape(1, -1)
    face_gain = face_gain.reshape(1, -1)
    owner, slot, block, area = (a.reshape(1, -1) for a in (owner, slot, block, area))
    operands = (state, flux, links, cells, face_gain, owner, slot, block, weight, area, gain)
    faces = cells.shape[1] // 4
    groups = blocks // GROUP
    dma = pltpu.SemaphoreType.DMA
    result, rates = pl.pallas_call(
        functools.partial(kernel, *mesh_shape),
        out_shape=(
            jax.ShapeDtypeStruct(state.shape, f32),
            jax.ShapeDtypeStruct(gain.shape, f32),
        ),
        in_specs=[pl.BlockSpec(memory_space=pl.ANY)] * len(operands),
        out_specs=(pl.BlockSpec(memory_space=pltpu.VMEM),) * 2,
        scratch_shapes=[pltpu.VMEM(a.shape, a.dtype) for a in operands]
        + [
            pltpu.VMEM((2 * rows, blocks), bf16),
            pltpu.VMEM((groups, slots * cell_rows, 256), bf16),
            pltpu.VMEM((groups, cell_rows, 256), f32),
            pltpu.VMEM((rows, blocks), f32),
            pltpu.VMEM((4, ROWS, faces), f32),
            pltpu.VMEM((4, ROWS, faces), f32),
            pltpu.VMEM((9, ROWS, PEL), f32),
            pltpu.VMEM((9, ROWS, PEL), f32),
            pltpu.VMEM((ROWS, PEL), f32),
            pltpu.VMEM((9, ROWS, PEL), f32),
            pltpu.VMEM((OWNER_PAIRS * 2 * ROWS, 2 * PEL), f32),
            pltpu.VMEM((OWNER_PAIRS * 2 * ROWS, 2 * PEL), bf16),
            dma((len(operands),)),
            dma((4,)),
            dma((4,)),
            dma((9,)),
            dma((9,)),
            dma((9,)),
            dma((9,)),
        ],
        compiler_params=pltpu.CompilerParams(
            collective_id=0, has_side_effects=True, vmem_limit_bytes=60 * 2**20
        ),
        name="bed_phase",
    )(*operands)
    return result[None, None], rates[None, None]


def solution(mesh):
    def spec(dims):
        return P("stream", "cross", *([None] * dims))

    return jax.shard_map(
        functools.partial(shards, (mesh.shape["stream"], mesh.shape["cross"])),
        mesh=mesh,
        in_specs=tuple(spec(d) for d in (3, 4, 2, 2, 2, 1, 1, 1, 2, 1, 2)),
        out_specs=(spec(3), spec(2)),
        check_vma=False,
    )
```

time: 549 us -> 79.9 us (0.15); the launches traced: 539 us -> 79.5 us
  matrix products: 210 us -> 0 us
  local copies, waits for them, and re-layouts: 196 us -> 8.66 us
  Pallas kernels: 0 us -> 70.2 us
  other arithmetic: 62.8 us -> 0 us
  starting transfers between devices: 33.1 us -> 0 us
  loops' own time: 29.5 us -> 0 us
  waiting for transfers between devices: 5.55 us -> 0 us
    dot_general x78 -> x0, matrix products: 210 us -> none  [the longest x16 83.8 us: deposit(): lax.dot_general(lookup, bin_table, (((1,), (1,)), ((), ())), precision=hi...]
    dynamic_slice x146 -> x0, local copies, waits for them, and re-layouts: 77.2 us -> none  [the longest x32 20.2 us: shards(): lax.scan(interpolate, jnp.zeros((R + 1, bin_count), jnp.float32), jnp.ara...]
    pallas_call x0 -> x1, Pallas kernels: none -> 70.2 us  [shards(): pl.pallas_call(functools.partial(kernel, *mesh_shape), out_shape=(jax.Sha...]
    squeeze x1 -> x0, local copies, waits for them, and re-layouts: 40.5 us -> none  [shards(): flux_blocks[0, 0]]
    convert_element_type x60 -> x0, other arithmetic: 39 us -> none  [the longest x16 16 us: deposit(): lax.dynamic_slice_in_dim(interp, first, step_len, 1).astype(jnp.float32)]
    ppermute x12 -> x0, starting transfers between devices: 33.1 us -> none  [the longest x4 15.8 us: padded(): lax.ppermute(lax.slice_in_dim(block, block.shape[dim] - width, None, axis...]
    another operation x4 -> x0, loops' own time: 29.5 us -> none  [the longest x1 11 us: shards(): lax.scan(interpolate, jnp.zeros((R + 1, bin_count), jnp.float32), jnp.ara...]
    while x128 -> x0, local copies, waits for them, and re-layouts: 25.6 us -> none
  transfers between devices with their start and end apart: 12 -> 0, of which waited for: 2 -> 0; matrix products, arithmetic and copies ran while one was open for 46% -> 0% of each run, Pallas kernels for 0% -> 0%
where the time goes in v1:
time: 79.9 us; the launch traced here: 79.5 us
  Pallas kernels  70.2 us (88%)
  local copies, waits for them, and re-layouts  8.66 us (11%)
    pallas_call x1, Pallas kernels, shards(): pl.pallas_call(functools.partial(kernel, *mesh_shape), out_shape=(jax.Sha...  70.2 us
    unnamed x6, local copies, waits for them, and re-layouts  8.66 us

profile of v1, /device:TPU:1, one launch (start us, length us, event | category | flops | bytes accessed | tf_op | source)
XLA Modules:
  0.0 79.5 jit_solution(14652408321524265333)
XLA Ops:
  0.6 1.3 %copy.21 = s32[1,1,7,256]{3,2,1,0:T(8,128)} copy(s32[1,1,7,256]{3,1,2,0:T(1,128)} %param.13) | data formatting | bytes 14336
  1.9 1.3 %copy.20 = f32[1,1,9,128]{3,2,1,0:T(8,128)} copy(f32[1,1,9,128]{3,1,2,0:T(1,128)} %param.21) | data formatting | bytes 9216
  3.2 1.4 %copy.16 = s32[1,1,4,1536]{3,1,2,0:T(1,128)} copy(s32[1,1,4,1536]{3,2,1,0:T(4,128)} %param.14) | data formatting | bytes 49152
  4.6 1.4 %copy.17 = f32[1,1,4,1536]{3,1,2,0:T(1,128)} copy(f32[1,1,4,1536]{3,2,1,0:T(4,128)} %param.15) | data formatting | bytes 49152
  5.9 70.2 %bed_phase.1 = (f32[12,64,256]{2,1,0:T(8,128)}, f32[9,128]{1,0:T(8,128)}) custom-call(f32[12,64,256]{2,1,0:T(8,128)} %bitcast.23, bf16[7,64,64,256]{3,2,1,0:T(8,128)(2,1)} %bitcast.21, s32[7,256]{1,0:T(8,128)} %bitcast.32, s32[1,6144]{1,0:T(1,128)} %bitcast.29, f32[1,6144]{1,0:T(1,128)} %bitcast.30, s32[1,32768]{1,0:T(1,128)} %bitcast.25, ...), custom_call_target="tpu_custom_call" | custom-call | tf_op jit(solution)/shard_map/bed_phase/pallas_call | solution.py:292
  76.1 1.3 %copy.13 = f32[1,1,9,128]{3,1,2,0:T(1,128)} copy(f32[1,1,9,128]{3,2,1,0:T(8,128)} %bitcast.33) | data formatting | bytes 9216
  77.4 2.1 %copy.23 = f32[1,1,12,64,256]{4,3,2,1,0:T(8,128)} copy(f32[1,1,12,64,256]{4,3,2,1,0:T(8,128)} %bitcast.24) | data formatting | bytes 1572864

commit v2 on v1

--- a/solution.py
+++ b/solution.py
@@ -10,7 +10,7 @@
 R = 9
 PEL = 128
 GROUP = 16
-POINT_STEP = 2048
+POINT_STEP = 4096
 FACE_STEP = 1536
 OWNER_PAIRS = 5
 ROWS = 16
@@ -50,7 +50,7 @@
     state_ref, flux_ref, links_ref, cells_ref, face_gain_ref, owner_ref, slot_ref, block_ref,
     weight_ref, area_ref, gain_ref,
     split_ref, coupled_ref, grouped_ref, total_ref,
-    face_out, face_in, part_out, part_in, rate_out, rate_in, binned_ref, table_ref,
+    face_out, face_in, part_out, part_in, rate_out, rate_in, binned_ref, last_ref, source_ref,
     in_sem, face_send, face_recv, part_send, part_recv, rate_send, rate_recv,
 ):
     s, x = lax.axis_index("stream"), lax.axis_index("cross")
@@ -58,7 +58,7 @@
     rows = components * cell_rows
     slots = flux_ref.shape[0]
     points = block_ref.shape[1]
-    faces = face_gain_ref.shape[1] // 4
+    faces = face_gain_ref.shape[1]
 
     def at(first, second):
         return (
@@ -89,13 +89,12 @@
     cell_iota = lax.broadcasted_iota(jnp.int32, (cell_rows, FACE_STEP), 0)
 
     def gather_faces(side, carry):
-        first = pl.multiple_of(side * faces, 128)
-        ids = cells_ref[0:1, pl.ds(first, FACE_STEP)]
+        ids = cells_ref[pl.ds(side, 1), :]
         table = one_hot(ids % blocks, blocks)
         both = dot(split_ref[...], table)
         chosen = both[:rows] + both[rows:]
         here = jnp.where((ids // blocks == cell_iota)[None], chosen.reshape(components, cell_rows, -1), 0.0)
-        gain = face_gain_ref[0:1, pl.ds(first, FACE_STEP)]
+        gain = face_gain_ref[pl.ds(side, 1), :]
         face_out[side, 0:components] = jnp.sum(here, axis=1) * gain
         face_out[side, components:ROWS] = jnp.zeros((ROWS - components, FACE_STEP), f32)
         return carry
@@ -170,7 +169,7 @@
     width = components * GROUP
 
     for k in range(slots):
-        table = one_hot(links_ref[k:k + 1, :], blocks)
+        table = one_hot(links_ref[k], blocks)
         coupled = dot(split_ref[0:rows], table).astype(bf16).reshape(components, cell_rows, blocks)
         for g in range(groups):
             lanes = slice(g * GROUP, (g + 1) * GROUP)
@@ -178,7 +177,7 @@
                 [coupled[q, :, lanes] for q in range(components)], axis=1
             )
 
-    step = 8
+    step = cell_rows // (points // POINT_STEP)
     mask = (
         lax.broadcasted_iota(jnp.int32, (1, GROUP, width), 2) % GROUP
         == lax.broadcasted_iota(jnp.int32, (1, GROUP, width), 1)
@@ -195,7 +194,6 @@
             grouped_ref[g, pl.ds(first, step), 0:width] = jnp.sum(jnp.where(mask, product, 0.0), axis=1)
         return carry
 
-    lax.fori_loop(0, cell_rows // step, couple, 0)
 
     totals = part_out[4]
     for copy in part_copies:
@@ -203,8 +201,10 @@
     for n in AROUND:
         totals = totals + part_in[n]
     mean = totals[0:R] / totals[R:R + 1]
-    rates = gain_ref[...] * mean / jnp.sqrt(1.0 + mean * mean)
-    rates_ref[...] = rates
+    gain = jnp.concatenate([gain_ref[r] for r in range(R)], axis=0)
+    rates = gain * mean / jnp.sqrt(1.0 + mean * mean)
+    for r in range(R):
+        rates_ref[r] = rates[r:r + 1]
     rate_out[0:R] = rates
     rate_out[R:ROWS] = jnp.zeros((ROWS - R, PEL), f32)
     rate_copies = [
@@ -221,10 +221,7 @@
     for copy in rate_copies:
         copy.start()
 
-    for q in range(components):
-        total_ref[q * cell_rows:(q + 1) * cell_rows] = jnp.concatenate(
-            [grouped_ref[g, :, q * GROUP:(q + 1) * GROUP] for g in range(groups)], axis=1
-        )
+    total_ref[...] = jnp.zeros_like(total_ref)
     for copy in face_copies:
         copy.wait()
     inside = [s > 0, s < stream_count - 1, x > 0, x < cross_count - 1]
@@ -233,8 +230,7 @@
         face_in[d] = face_in[d] * present[d] - face_out[d]
 
     def add_faces(side, carry):
-        first = pl.multiple_of(side * faces, 128)
-        ids = cells_ref[0:1, pl.ds(first, FACE_STEP)]
+        ids = cells_ref[pl.ds(side, 1), :]
         table = one_hot(ids % blocks, blocks)
         here = ids // blocks == cell_iota
         net = face_in[side, 0:components]
@@ -248,32 +244,43 @@
     rate_in[4] = rate_out[...]
     for copy in rate_copies:
         copy.wait()
+    last_ref[...] = jnp.zeros_like(last_ref)
     for n in range(9):
-        first = (n // 2) * 2 * ROWS
-        lanes = slice((n % 2) * PEL, (n % 2 + 1) * PEL)
-        high, low = split(rate_in[n])
-        table_ref[first:first + ROWS, lanes] = high
-        table_ref[first + ROWS:first + 2 * ROWS, lanes] = low
-    table_ref[8 * ROWS:10 * ROWS, PEL:2 * PEL] = jnp.zeros((2 * ROWS, PEL), bf16)
-
-    def deposit(step, carry):
-        first = pl.multiple_of(step * POINT_STEP, POINT_STEP)
-        pair, pellets = pellet_code(first)
-        found = dot(table_ref[...], pellets)
-        source = jnp.zeros((ROWS, POINT_STEP), f32)
-        for g in range(OWNER_PAIRS):
-            top = g * 2 * ROWS
-            rate = found[top:top + ROWS] + found[top + ROWS:top + 2 * ROWS]
-            source = jnp.where(pair == g, rate, source)
-        source = source * area_ref[0:1, pl.ds(first, POINT_STEP)]
+        last_ref[n:n + 1] = rate_in[n, R - 1:R]
+    code = lax.broadcasted_iota(jnp.int32, (ROWS, PEL), 0)
+
+    def look_up(first):
+        owner = jnp.broadcast_to(owner_ref[0:1, pl.ds(first, PEL)], (8, PEL))
+        slot = jnp.broadcast_to(slot_ref[0:1, pl.ds(first, PEL)], (8, PEL))
+        found = jnp.zeros((8, PEL), f32)
+        for n in range(9):
+            found = jnp.where(owner == n, jnp.take_along_axis(rate_in[n, 0:8], slot, axis=1), found)
+        last = jnp.where(owner == code[0:8], jnp.take_along_axis(last_ref[0:8], slot, axis=1), 0.0)
+        last = last + jnp.where(owner == code[8:ROWS], jnp.take_along_axis(last_ref[8:ROWS], slot, axis=1), 0.0)
+        area = area_ref[0:1, pl.ds(first, PEL)]
+        return found * area, jnp.sum(last, axis=0, keepdims=True) * area
+
+    def deposit(which, carry):
+        first = pl.multiple_of(which * POINT_STEP, POINT_STEP)
+        for n in range(POINT_STEP // PEL):
+            lanes = slice(n * PEL, (n + 1) * PEL)
+            most, last = look_up(first + n * PEL)
+            source_ref[0:8, lanes] = most
+            source_ref[8:9, lanes] = last
+        source = source_ref[...]
         table = one_hot(block_ref[0:1, pl.ds(first, POINT_STEP)], blocks)
         weights = weight_ref[:, pl.ds(first, POINT_STEP)].astype(f32)
         spread = (weights[None] * source[0:R, None, :]).astype(bf16).reshape(R * cell_rows, POINT_STEP)
         total_ref[0:R * cell_rows] += dot_t(spread, table)
-        return carry
+        return couple(which, carry)
 
     lax.fori_loop(0, points // POINT_STEP, deposit, 0)
-    next_ref[...] = state_ref[...] + phase_dt * total_ref[...].reshape(components, cell_rows, blocks)
+    for q in range(components):
+        interior = jnp.concatenate(
+            [grouped_ref[g, :, q * GROUP:(q + 1) * GROUP] for g in range(groups)], axis=1
+        )
+        added = total_ref[q * cell_rows:(q + 1) * cell_rows]
+        next_ref[q] = state_ref[q] + phase_dt * (interior + added)
 
 
 def shards(mesh_shape, *arrays):
@@ -282,11 +289,11 @@
     components, cell_rows, blocks = state.shape
     slots = flux.shape[0]
     rows = components * cell_rows
-    cells = cells.reshape(1, -1)
-    face_gain = face_gain.reshape(1, -1)
+    links = links[:, None]
+    gain = gain[:, None]
     owner, slot, block, area = (a.reshape(1, -1) for a in (owner, slot, block, area))
     operands = (state, flux, links, cells, face_gain, owner, slot, block, weight, area, gain)
-    faces = cells.shape[1] // 4
+    faces = cells.shape[1]
     groups = blocks // GROUP
     dma = pltpu.SemaphoreType.DMA
     result, rates = pl.pallas_call(
@@ -310,7 +317,8 @@
             pltpu.VMEM((ROWS, PEL), f32),
             pltpu.VMEM((9, ROWS, PEL), f32),
             pltpu.VMEM((OWNER_PAIRS * 2 * ROWS, 2 * PEL), f32),
-            pltpu.VMEM((OWNER_PAIRS * 2 * ROWS, 2 * PEL), bf16),
+            pltpu.VMEM((ROWS, PEL), f32),
+            pltpu.VMEM((ROWS, POINT_STEP), f32),
             dma((len(operands),)),
             dma((4,)),
             dma((4,)),
@@ -324,7 +332,7 @@
         ),
         name="bed_phase",
     )(*operands)
-    return result[None, None], rates[None, None]
+    return result[None, None], rates[None, None, :, 0]
 
 
 def solution(mesh):

time: 79.9 us -> 67.1 us (0.84)
  Pallas kernels: 70.2 us -> 63 us
  local copies, waits for them, and re-layouts: 8.66 us -> 3.34 us
    pallas_call x1, Pallas kernels: 70.2 us -> 63 us  [shards(): pl.pallas_call(functools.partial(kernel, *mesh_shape), out_shape=(jax.Sha...]
    unnamed x6 -> x2, local copies, waits for them, and re-layouts: 8.66 us -> 3.34 us
where the time goes in v2:
time: 67.1 us; the launch traced here: 66.9 us
  Pallas kernels  63 us (94%)
  local copies, waits for them, and re-layouts  3.34 us (5%)
    pallas_call x1, Pallas kernels, shards(): pl.pallas_call(functools.partial(kernel, *mesh_shape), out_shape=(jax.Sha...  63 us
    unnamed x2, local copies, waits for them, and re-layouts  3.34 us

profile of v2, /device:TPU:1, one launch (start us, length us, event | category | flops | bytes accessed | tf_op | source)
XLA Modules:
  0.0 66.9 jit_solution(461187879144146614)
XLA Ops:
  0.6 63.0 %bed_phase.1 = (f32[12,64,256]{2,1,0:T(8,128)}, f32[9,1,128]{2,1,0:T(1,128)}) custom-call(f32[12,64,256]{2,1,0:T(8,128)} %bitcast.17, bf16[7,64,64,256]{3,2,1,0:T(8,128)(2,1)} %bitcast.15, s32[7,1,256]{2,1,0:T(1,128)} %bitcast.25, s32[4,1536]{1,0:T(4,128)} %bitcast.23, f32[4,1536]{1,0:T(4,128)} %bitcast.24, s32[1,32768]{1,0:T(1,128)} %bitcast.19, ...), custom_call_target="tpu_custom_call" | custom-call | tf_op jit(solution)/shard_map/bed_phase/pallas_call | solution.py:299
  63.6 2.1 %copy.16 = f32[1,1,12,64,256]{4,3,2,1,0:T(8,128)} copy(f32[1,1,12,64,256]{4,3,2,1,0:T(8,128)} %bitcast.18) | data formatting | bytes 1572864
  65.7 1.3 %copy.17 = f32[1,1,9,128]{3,1,2,0:T(1,128)} copy(f32[1,1,9,128]{3,1,2,0:T(1,128)} %bitcast.27) | data formatting | bytes 9216

commit v3 on v2

--- a/solution.py
+++ b/solution.py
@@ -14,6 +14,7 @@
 FACE_STEP = 1536
 OWNER_PAIRS = 5
 ROWS = 16
+PARTS = 2
 
 phase_dt = 0.5
 f32 = jnp.float32
@@ -41,15 +42,28 @@
     return lax.dot_general(a, b, (((1,), (1,)), ((), ())), preferred_element_type=f32)
 
 
+def swap_parts(arrays):
+    arrays = list(arrays)
+    lane = lax.broadcasted_iota(jnp.int32, arrays[0].shape, 1) // GROUP
+    for far in (4, 2, 1):
+        low = (lane & far).astype(f32).astype(arrays[0].dtype) == 0
+        for n in range(8):
+            if n & far == 0:
+                a, b = arrays[n], arrays[n + far]
+                arrays[n] = jnp.where(low, a, jnp.roll(b, far * GROUP, axis=1))
+                arrays[n + far] = jnp.where(low, jnp.roll(a, -far * GROUP, axis=1), b)
+    return arrays
+
+
 def kernel(
     stream_count,
     cross_count,
     state_hbm, flux_hbm, links_hbm, cells_hbm, face_gain_hbm, owner_hbm, slot_hbm, block_hbm,
     weight_hbm, area_hbm, gain_hbm,
-    next_ref, rates_ref,
+    change_ref, rates_ref,
     state_ref, flux_ref, links_ref, cells_ref, face_gain_ref, owner_ref, slot_ref, block_ref,
     weight_ref, area_ref, gain_ref,
-    split_ref, coupled_ref, grouped_ref, total_ref,
+    split_ref, coupled_ref, interior_ref, total_ref,
     face_out, face_in, part_out, part_in, rate_out, rate_in, binned_ref, last_ref, source_ref,
     in_sem, face_send, face_recv, part_send, part_recv, rate_send, rate_recv,
 ):
@@ -116,7 +130,7 @@
     for copy in face_copies:
         copy.start()
 
-    for load in loads[3:8]:
+    for load in loads[3:9]:
         load.wait()
     binned_ref[...] = jnp.zeros_like(binned_ref)
 
@@ -124,6 +138,20 @@
         owner = owner_ref[0:1, pl.ds(first, POINT_STEP)]
         slot = slot_ref[0:1, pl.ds(first, POINT_STEP)]
         return owner // 2, one_hot((owner % 2) * PEL + slot, 2 * PEL)
+
+    groups = blocks // GROUP
+    width = 256
+
+    def arrange(k):
+        table = one_hot(links_ref[k], blocks)
+        coupled = dot(split_ref[0:rows], table).astype(bf16).reshape(components, cell_rows, blocks)
+        place = pl.ds(pl.multiple_of(k * cell_rows, cell_rows), cell_rows)
+        halves = [[coupled[q, :, h * 128:(h + 1) * 128] for q in range(components)] for h in range(2)]
+        rest = swap_parts(halves[0][8:] + halves[1][8:])
+        for h in range(2):
+            for d, part in enumerate(swap_parts(halves[h][:8])):
+                coupled_ref[h * 8 + d, place, 0:128] = part
+                coupled_ref[h * 8 + d, place, 128:256] = rest[d]
 
     def interpolate(step, carry):
         first = pl.multiple_of(step * POINT_STEP, POINT_STEP)
@@ -140,6 +168,7 @@
         both = jnp.concatenate([high.astype(f32), low.astype(f32)], axis=0)
         masked = jnp.concatenate([jnp.where(pair == g, both, 0.0) for g in range(OWNER_PAIRS)], axis=0)
         binned_ref[...] += dot_t(masked.astype(bf16), pellets)
+        arrange(jnp.minimum(step, slots - 1))
         return carry
 
     lax.fori_loop(0, points // POINT_STEP, interpolate, 0)
@@ -163,20 +192,8 @@
     for copy in part_copies:
         copy.start()
 
-    for load in loads[8:]:
+    for load in loads[9:]:
         load.wait()
-    groups = blocks // GROUP
-    width = components * GROUP
-
-    for k in range(slots):
-        table = one_hot(links_ref[k], blocks)
-        coupled = dot(split_ref[0:rows], table).astype(bf16).reshape(components, cell_rows, blocks)
-        for g in range(groups):
-            lanes = slice(g * GROUP, (g + 1) * GROUP)
-            coupled_ref[g, k * cell_rows:(k + 1) * cell_rows, 0:width] = jnp.concatenate(
-                [coupled[q, :, lanes] for q in range(components)], axis=1
-            )
-
     step = cell_rows // (points // POINT_STEP)
     mask = (
         lax.broadcasted_iota(jnp.int32, (1, GROUP, width), 2) % GROUP
@@ -188,12 +205,41 @@
         turned = [
             jnp.transpose(flux_ref[:, first + n].reshape(slots * cell_rows, blocks)) for n in range(step)
         ]
+        found = []
         for g in range(groups):
             left = jnp.concatenate([t[g * GROUP:(g + 1) * GROUP] for t in turned], axis=0)
-            product = dot(left, coupled_ref[g, :, 0:width]).reshape(step, GROUP, width)
-            grouped_ref[g, pl.ds(first, step), 0:width] = jnp.sum(jnp.where(mask, product, 0.0), axis=1)
-        return carry
-
+            product = dot(left, coupled_ref[g]).reshape(step, GROUP, width)
+            found.append(jnp.sum(jnp.where(mask, product, 0.0), axis=1))
+        for h in range(2):
+            for q, part in enumerate(swap_parts([found[h * 8 + d][:, 0:128] for d in range(8)])):
+                interior_ref[q, pl.ds(first, step), h * 128:(h + 1) * 128] = part
+        front = lax.broadcasted_iota(jnp.int32, (step, 128), 1) < 64
+        rest = [jnp.where(front, found[d][:, 128:256], found[8 + d][:, 128:256]) for d in range(8)]
+        for n, part in enumerate(swap_parts(rest)):
+            h = n // 4
+            interior_ref[8 + n % 4, pl.ds(first, step), h * 128:(h + 1) * 128] = part
+        return carry
+
+
+    total_ref[...] = jnp.zeros_like(total_ref)
+    for copy in face_copies:
+        copy.wait()
+    inside = [s > 0, s < stream_count - 1, x > 0, x < cross_count - 1]
+    present = [jnp.where(here, 1.0, 0.0) for here in inside]
+    for d in range(4):
+        face_in[d] = face_in[d] * present[d] - face_out[d]
+
+    def add_faces(side, carry):
+        ids = cells_ref[pl.ds(side, 1), :]
+        table = one_hot(ids % blocks, blocks)
+        here = ids // blocks == cell_iota
+        net = face_in[side, 0:components]
+        spread = jnp.where(here[None], net[:, None, :], 0.0).reshape(rows, FACE_STEP)
+        high, low = split(spread)
+        total_ref[...] += dot_t(high, table) + dot_t(low, table)
+        return carry
+
+    lax.fori_loop(0, 2, add_faces, 0)
 
     totals = part_out[4]
     for copy in part_copies:
@@ -221,25 +267,7 @@
     for copy in rate_copies:
         copy.start()
 
-    total_ref[...] = jnp.zeros_like(total_ref)
-    for copy in face_copies:
-        copy.wait()
-    inside = [s > 0, s < stream_count - 1, x > 0, x < cross_count - 1]
-    present = [jnp.where(here, 1.0, 0.0) for here in inside]
-    for d in range(4):
-        face_in[d] = face_in[d] * present[d] - face_out[d]
-
-    def add_faces(side, carry):
-        ids = cells_ref[pl.ds(side, 1), :]
-        table = one_hot(ids % blocks, blocks)
-        here = ids // blocks == cell_iota
-        net = face_in[side, 0:components]
-        spread = jnp.where(here[None], net[:, None, :], 0.0).reshape(rows, FACE_STEP)
-        high, low = split(spread)
-        total_ref[...] += dot_t(high, table) + dot_t(low, table)
-        return carry
-
-    lax.fori_loop(0, 4, add_faces, 0)
+    lax.fori_loop(2, 4, add_faces, 0)
 
     rate_in[4] = rate_out[...]
     for copy in rate_copies:
@@ -260,27 +288,35 @@
         area = area_ref[0:1, pl.ds(first, PEL)]
         return found * area, jnp.sum(last, axis=0, keepdims=True) * area
 
-    def deposit(which, carry):
+    def look_up_step(which, half):
         first = pl.multiple_of(which * POINT_STEP, POINT_STEP)
         for n in range(POINT_STEP // PEL):
             lanes = slice(n * PEL, (n + 1) * PEL)
             most, last = look_up(first + n * PEL)
-            source_ref[0:8, lanes] = most
-            source_ref[8:9, lanes] = last
-        source = source_ref[...]
+            source_ref[half, 0:8, lanes] = most
+            source_ref[half, 8:9, lanes] = last
+
+    def deposit(which, carry):
+        first = pl.multiple_of(which * POINT_STEP, POINT_STEP)
+        source = source_ref[lax.rem(which, 2)]
         table = one_hot(block_ref[0:1, pl.ds(first, POINT_STEP)], blocks)
         weights = weight_ref[:, pl.ds(first, POINT_STEP)].astype(f32)
         spread = (weights[None] * source[0:R, None, :]).astype(bf16).reshape(R * cell_rows, POINT_STEP)
         total_ref[0:R * cell_rows] += dot_t(spread, table)
-        return couple(which, carry)
-
+        couple(which, carry)
+        look_up_step(jnp.minimum(which + 1, points // POINT_STEP - 1), lax.rem(which + 1, 2))
+        return carry
+
+    look_up_step(0, 0)
     lax.fori_loop(0, points // POINT_STEP, deposit, 0)
     for q in range(components):
-        interior = jnp.concatenate(
-            [grouped_ref[g, :, q * GROUP:(q + 1) * GROUP] for g in range(groups)], axis=1
-        )
         added = total_ref[q * cell_rows:(q + 1) * cell_rows]
-        next_ref[q] = state_ref[q] + phase_dt * (interior + added)
+        change_ref[q] = interior_ref[q] + added
+
+
+def advance(state_ref, change_ref, found_ref, next_ref, rates_ref):
+    next_ref[...] = state_ref[...] + phase_dt * change_ref[...]
+    rates_ref[...] = found_ref[...]
 
 
 def shards(mesh_shape, *arrays):
@@ -296,7 +332,7 @@
     faces = cells.shape[1]
     groups = blocks // GROUP
     dma = pltpu.SemaphoreType.DMA
-    result, rates = pl.pallas_call(
+    change, found = pl.pallas_call(
         functools.partial(kernel, *mesh_shape),
         out_shape=(
             jax.ShapeDtypeStruct(state.shape, f32),
@@ -308,7 +344,7 @@
         + [
             pltpu.VMEM((2 * rows, blocks), bf16),
             pltpu.VMEM((groups, slots * cell_rows, 256), bf16),
-            pltpu.VMEM((groups, cell_rows, 256), f32),
+            pltpu.VMEM(state.shape, f32),
             pltpu.VMEM((rows, blocks), f32),
             pltpu.VMEM((4, ROWS, faces), f32),
             pltpu.VMEM((4, ROWS, faces), f32),
@@ -318,7 +354,7 @@
             pltpu.VMEM((9, ROWS, PEL), f32),
             pltpu.VMEM((OWNER_PAIRS * 2 * ROWS, 2 * PEL), f32),
             pltpu.VMEM((ROWS, PEL), f32),
-            pltpu.VMEM((ROWS, POINT_STEP), f32),
+            pltpu.VMEM((2, ROWS, POINT_STEP), f32),
             dma((len(operands),)),
             dma((4,)),
             dma((4,)),
@@ -332,6 +368,19 @@
         ),
         name="bed_phase",
     )(*operands)
+    whole = pl.BlockSpec(gain.shape, lambda n: (0, 0, 0))
+    part = pl.BlockSpec((components // PARTS,) + state.shape[1:], lambda n: (n, 0, 0))
+    result, rates = pl.pallas_call(
+        advance,
+        grid=(PARTS,),
+        out_shape=(
+            jax.ShapeDtypeStruct(state.shape, f32),
+            jax.ShapeDtypeStruct(gain.shape, f32),
+        ),
+        in_specs=[part, part, whole],
+        out_specs=(part, whole),
+        name="advance",
+    )(state, change, found)
     return result[None, None], rates[None, None, :, 0]
 
 

time: 67.1 us -> 62.2 us (0.927)
  local copies, waits for them, and re-layouts: 3.34 us -> 0 us
  Pallas kernels: 63 us -> 61.4 us
    pallas_call x1, Pallas kernels: 63 us -> 59.3 us  [shards(): pl.pallas_call(functools.partial(kernel, *mesh_shape), out_shape=(jax.Sha...]
    unnamed x2 -> x0, local copies, waits for them, and re-layouts: 3.34 us -> none
    pallas_call x0 -> x1, Pallas kernels: none -> 2.18 us  [shards(): pl.pallas_call(advance, grid=(PARTS,), out_shape=(jax.ShapeDtypeStruct(st...]
where the time goes in v3:
time: 62.2 us; the launch traced here: 62.1 us
  Pallas kernels  61.4 us (99%)
  between operations  0.64 us (1%)
    pallas_call x1, Pallas kernels, shards(): pl.pallas_call(functools.partial(kernel, *mesh_shape), out_shape=(jax.Sha...  59.3 us
    pallas_call x1, Pallas kernels, shards(): pl.pallas_call(advance, grid=(PARTS,), out_shape=(jax.ShapeDtypeStruct(st...  2.18 us

profile of v3, /device:TPU:1, one launch (start us, length us, event | category | flops | bytes accessed | tf_op | source)
XLA Modules:
  0.0 62.1 jit_solution(14612950908629507810)
XLA Ops:
  0.6 59.3 %bed_phase.1 = (f32[12,64,256]{2,1,0:T(8,128)}, f32[9,1,128]{2,1,0:T(1,128)}) custom-call(f32[12,64,256]{2,1,0:T(8,128)} %bitcast.17, bf16[7,64,64,256]{3,2,1,0:T(8,128)(2,1)} %bitcast.15, s32[7,1,256]{2,1,0:T(1,128)} %bitcast.25, s32[4,1536]{1,0:T(4,128)} %bitcast.23, f32[4,1536]{1,0:T(4,128)} %bitcast.24, s32[1,32768]{1,0:T(1,128)} %bitcast.19, ...), custom_call_target="tpu_custom_call" | custom-call | tf_op jit(solution)/shard_map/bed_phase/pallas_call | solution.py:335
  59.9 2.2 %advance.1 = (f32[12,64,256]{2,1,0:T(8,128)}, f32[9,1,128]{2,1,0:T(1,128)}) custom-call(f32[12,64,256]{2,1,0:T(8,128)} %bitcast.18, f32[12,64,256]{2,1,0:T(8,128)} %get-tuple-element.6.change_ref, f32[9,1,128]{2,1,0:T(1,128)} %get-tuple-element.7.found_ref), custom_call_target="tpu_custom_call" | custom-call | tf_op jit(solution)/shard_map/advance/pallas_call | solution.py:373

commit v4 on v3

--- a/solution.py
+++ b/solution.py
@@ -10,7 +10,7 @@
 R = 9
 PEL = 128
 GROUP = 16
-POINT_STEP = 4096
+POINT_STEP = 8192
 FACE_STEP = 1536
 OWNER_PAIRS = 5
 ROWS = 16
@@ -168,7 +168,8 @@
         both = jnp.concatenate([high.astype(f32), low.astype(f32)], axis=0)
         masked = jnp.concatenate([jnp.where(pair == g, both, 0.0) for g in range(OWNER_PAIRS)], axis=0)
         binned_ref[...] += dot_t(masked.astype(bf16), pellets)
-        arrange(jnp.minimum(step, slots - 1))
+        for n in range(2):
+            arrange(jnp.minimum(2 * step + n, slots - 1))
         return carry
 
     lax.fori_loop(0, points // POINT_STEP, interpolate, 0)

time: 62.2 us -> 59.9 us (0.963)
  Pallas kernels: 61.4 us -> 59.1 us
    pallas_call x1, Pallas kernels: 59.3 us -> 56.9 us  [shards(): pl.pallas_call(functools.partial(kernel, *mesh_shape), out_shape=(jax.Sha...]
where the time goes in v4:
time: 59.9 us; the launch traced here: 59.7 us
  Pallas kernels  59.1 us (99%)
  between operations  0.64 us (1%)
    pallas_call x1, Pallas kernels, shards(): pl.pallas_call(functools.partial(kernel, *mesh_shape), out_shape=(jax.Sha...  56.9 us
    pallas_call x1, Pallas kernels, shards(): pl.pallas_call(advance, grid=(PARTS,), out_shape=(jax.ShapeDtypeStruct(st...  2.18 us

profile of v4, /device:TPU:1, one launch (start us, length us, event | category | flops | bytes accessed | tf_op | source)
XLA Modules:
  0.0 59.7 jit_solution(15846822888390854728)
XLA Ops:
  0.6 56.9 %bed_phase.1 = (f32[12,64,256]{2,1,0:T(8,128)}, f32[9,1,128]{2,1,0:T(1,128)}) custom-call(f32[12,64,256]{2,1,0:T(8,128)} %bitcast.17, bf16[7,64,64,256]{3,2,1,0:T(8,128)(2,1)} %bitcast.15, s32[7,1,256]{2,1,0:T(1,128)} %bitcast.25, s32[4,1536]{1,0:T(4,128)} %bitcast.23, f32[4,1536]{1,0:T(4,128)} %bitcast.24, s32[1,32768]{1,0:T(1,128)} %bitcast.19, ...), custom_call_target="tpu_custom_call" | custom-call | tf_op jit(solution)/shard_map/bed_phase/pallas_call | solution.py:336
  57.5 2.2 %advance.1 = (f32[12,64,256]{2,1,0:T(8,128)}, f32[9,1,128]{2,1,0:T(1,128)}) custom-call(f32[12,64,256]{2,1,0:T(8,128)} %bitcast.18, f32[12,64,256]{2,1,0:T(8,128)} %get-tuple-element.6.change_ref, f32[9,1,128]{2,1,0:T(1,128)} %get-tuple-element.7.found_ref), custom_call_target="tpu_custom_call" | custom-call | tf_op jit(solution)/shard_map/advance/pallas_call | solution.py:374

commit v5 on v4

--- a/solution.py
+++ b/solution.py
@@ -86,7 +86,7 @@
         (weight_hbm, weight_ref), (links_hbm, links_ref), (gain_hbm, gain_ref), (flux_hbm, flux_ref),
     ]
     loads = [pltpu.make_async_copy(a, b, in_sem.at[n]) for n, (a, b) in enumerate(pairs)]
-    for load in loads:
+    for load in loads[:-1]:
         load.start()
     barrier = pltpu.get_barrier_semaphore()
     for n in AROUND:
@@ -114,6 +114,7 @@
         return carry
 
     lax.fori_loop(0, 4, gather_faces, 0)
+    loads[-1].start()
     pl.semaphore_wait(barrier, len(AROUND))
     sides = [(-1, 0, 1), (1, 0, 0), (0, -1, 3), (0, 1, 2)]
     face_copies = [
@@ -196,10 +197,21 @@
     for load in loads[9:]:
         load.wait()
     step = cell_rows // (points // POINT_STEP)
-    mask = (
-        lax.broadcasted_iota(jnp.int32, (1, GROUP, width), 2) % GROUP
-        == lax.broadcasted_iota(jnp.int32, (1, GROUP, width), 1)
-    )
+    lane = lax.broadcasted_iota(jnp.int32, (8, 128), 1)
+    row = lax.broadcasted_iota(jnp.int32, (8, 128), 0)
+
+    def diagonal(product):
+        merged = None
+        for n in range(8):
+            top = product[n * GROUP:n * GROUP + 8]
+            here = jnp.where(lane % GROUP < 8, top, product[n * GROUP + 8:(n + 1) * GROUP])
+            if n == 0:
+                merged = here
+            else:
+                merged = jnp.where(row == (lane + n) % 8, pltpu.roll(here, n, 0), merged)
+        for far in (1, 2, 4):
+            merged = jnp.where(lane & far == 0, merged, pltpu.roll(merged, 8 - far, 0))
+        return merged
 
     def couple(which, carry):
         first = pl.multiple_of(which * step, step)
@@ -209,13 +221,19 @@
         found = []
         for g in range(groups):
             left = jnp.concatenate([t[g * GROUP:(g + 1) * GROUP] for t in turned], axis=0)
-            product = dot(left, coupled_ref[g]).reshape(step, GROUP, width)
-            found.append(jnp.sum(jnp.where(mask, product, 0.0), axis=1))
+            product = dot(left, coupled_ref[g])
+            found.append([
+                jnp.concatenate([
+                    diagonal(product[n * GROUP:(n + 8) * GROUP, h * 128:(h + 1) * 128])
+                    for n in range(0, step, 8)
+                ], axis=0)
+                for h in range(2)
+            ])
         for h in range(2):
-            for q, part in enumerate(swap_parts([found[h * 8 + d][:, 0:128] for d in range(8)])):
+            for q, part in enumerate(swap_parts([found[h * 8 + d][0] for d in range(8)])):
                 interior_ref[q, pl.ds(first, step), h * 128:(h + 1) * 128] = part
         front = lax.broadcasted_iota(jnp.int32, (step, 128), 1) < 64
-        rest = [jnp.where(front, found[d][:, 128:256], found[8 + d][:, 128:256]) for d in range(8)]
+        rest = [jnp.where(front, found[d][1], found[8 + d][1]) for d in range(8)]
         for n, part in enumerate(swap_parts(rest)):
             h = n // 4
             interior_ref[8 + n % 4, pl.ds(first, step), h * 128:(h + 1) * 128] = part

time: 59.9 us -> 59.9 us (level)
  no operation moved by 1% of the time
where the time goes in v5:
time: 59.9 us; the launch traced here: 59.7 us
  Pallas kernels  59.1 us (99%)
  between operations  0.64 us (1%)
    pallas_call x1, Pallas kernels, shards(): pl.pallas_call(functools.partial(kernel, *mesh_shape), out_shape=(jax.Sha...  56.9 us
    pallas_call x1, Pallas kernels, shards(): pl.pallas_call(advance, grid=(PARTS,), out_shape=(jax.ShapeDtypeStruct(st...  2.18 us

profile of v5, /device:TPU:1, one launch (start us, length us, event | category | flops | bytes accessed | tf_op | source)
XLA Modules:
  0.0 59.7 jit_solution(17696928135630323186)
XLA Ops:
  0.6 56.9 %bed_phase.1 = (f32[12,64,256]{2,1,0:T(8,128)}, f32[9,1,128]{2,1,0:T(1,128)}) custom-call(f32[12,64,256]{2,1,0:T(8,128)} %bitcast.17, bf16[7,64,64,256]{3,2,1,0:T(8,128)(2,1)} %bitcast.15, s32[7,1,256]{2,1,0:T(1,128)} %bitcast.25, s32[4,1536]{1,0:T(4,128)} %bitcast.23, f32[4,1536]{1,0:T(4,128)} %bitcast.24, s32[1,32768]{1,0:T(1,128)} %bitcast.19, ...), custom_call_target="tpu_custom_call" | custom-call | tf_op jit(solution)/shard_map/bed_phase/pallas_call | solution.py:354
  57.5 2.2 %advance.1 = (f32[12,64,256]{2,1,0:T(8,128)}, f32[9,1,128]{2,1,0:T(1,128)}) custom-call(f32[12,64,256]{2,1,0:T(8,128)} %bitcast.18, f32[12,64,256]{2,1,0:T(8,128)} %get-tuple-element.6.change_ref, f32[9,1,128]{2,1,0:T(1,128)} %get-tuple-element.7.found_ref), custom_call_target="tpu_custom_call" | custom-call | tf_op jit(solution)/shard_map/advance/pallas_call | solution.py:392
